TPU v7x, 32 devices: a whole 2x2x4 slice. The times are simulated.
32 devices in a mesh: section: 2 (over y), seq: 8 (over z, core), dp: 2 (over x).
Axes of the slice: x: 2, y: 2, z: 4, core: 2. Of those that a mesh axis runs over, the one named last changes fastest.
Arguments:
- mel: bfloat16 [4, 4096, 128], P('dp', 'seq'), may hold values from -6 to 6
- lengths: int32 [4], P('dp'), may hold values from 512 to 1024, as said below
- stem_weight: bfloat16 [512, 1536], P(('seq', 'dp')), may hold values from -0.25 to 0.25
- w_qkv: bfloat16 [2, 1536, 2304], P('section', ('seq', 'dp'))
- w_out: bfloat16 [2, 768, 1536], P('section', ('seq', 'dp')), may hold values from -0.21875 to 0.21875
- norm_gains: float32 [2, 2, 1536], P('section'), may hold values from 0.25 to 1.75
- conv_kernel: float32 [2, 5, 1536], P('section'), may hold values from -2.5 to 2.5
Outputs:
- arrivals: bfloat16 [2, 4, 1024, 1536], P('section', 'dp', 'seq')
Inputs may be any that keep to these rules, and one draw needn't show every extreme that they name: `lengths`: every utterance keeps at least half of its 1024 frames; one utterance of each draw keeps all of them.
All inputs are finite; a program needn't handle non-finite values.
Results may differ from a plain program's by a relative error of at most 0.029.
Values may be sent and summed in bfloat16 or wider, within the bound.
No kernel may reach another device: no remote copies, remote signals or barrier semaphores. Data moves between devices by JAX's collectives and lax.ppermute only.
A program may use at most 64 MiB of HBM per device.

v0:
```python
import jax
import jax.numpy as jnp
from jax import lax
from jax.sharding import PartitionSpec as P

HEADS = 8
STRIDE = 4


eps = 1e-05
masked_score = -1e30


def extended(block, sides, width):
    for axis, dim in sides:
        count = lax.axis_size(axis)
        forward = [(i, i + 1) for i in range(count - 1)]
        backward = [(target, source) for source, target in forward]
        low = lax.ppermute(
            lax.slice_in_dim(block, block.shape[dim] - width, None, axis=dim), axis, forward
        )
        high = lax.ppermute(lax.slice_in_dim(block, 0, width, axis=dim), axis, backward)
        block = jnp.concatenate([low, block, high], axis=dim)
    return block


def from_behind(value, axis, steps):
    count = lax.axis_size(axis)
    pairs = [(source, (source + steps) % count) for source in range(count)]
    return lax.ppermute(value, axis, pairs)


def layer_norm(value, gain):
    average = jnp.mean(value, axis=-1, keepdims=True)
    centered = value - average
    variance = jnp.mean(centered * centered, axis=-1, keepdims=True)
    return centered * lax.rsqrt(variance + eps) * gain


def band_attention(queries, keys_values, first_query, length, heads):
    frames = queries.shape[0]
    width = queries.shape[1]
    head_size = width // heads
    span = keys_values.shape[0]
    query_rows = queries.reshape(frames, heads, head_size)
    key_rows = keys_values[:, :width].reshape(span, heads, head_size)
    value_rows = keys_values[:, width:].reshape(span, heads, head_size)
    scores = jnp.einsum(
        "qhd,khd->hqk", query_rows, key_rows, preferred_element_type=jnp.float32
    ) * (1.0 / head_size**0.5)
    query_pos = first_query + jnp.arange(frames, dtype=jnp.int32)
    key_pos = first_query - frames + jnp.arange(span, dtype=jnp.int32)
    allowed = (
        (key_pos[None, :] >= 0)
        & (key_pos[None, :] < length)
        & (jnp.abs(query_pos[:, None] - key_pos[None, :]) <= frames)
    )
    scores = jnp.where(allowed[None], scores, masked_score)
    highest = jnp.max(scores, axis=-1, keepdims=True)
    expon = jnp.exp(scores - highest)
    probs = (expon / jnp.sum(expon, axis=-1, keepdims=True)).astype(jnp.bfloat16)
    context = jnp.einsum("hqk,khd->qhd", probs, value_rows, preferred_element_type=jnp.float32)
    return context.astype(jnp.bfloat16).reshape(frames, width)


def apply_layer(held_input, valid, length, first_query, full_qkv, full_out, gains, kernel):
    frames = held_input.shape[0]
    width = full_out.shape[0]
    stream = held_input.astype(jnp.float32)
    normed = layer_norm(stream, gains[0]).astype(jnp.bfloat16)
    qkv = jnp.dot(normed, full_qkv, preferred_element_type=jnp.float32).astype(jnp.bfloat16)
    nearby = extended(qkv[:, width:], (("seq", 0),), frames)
    context = band_attention(qkv[:, :width], nearby, first_query, length, HEADS)
    stream = stream + jnp.dot(context, full_out, preferred_element_type=jnp.float32)
    conv_in = (layer_norm(stream, gains[1]) * valid[:, None]).astype(jnp.bfloat16)
    taps = kernel.shape[0]
    padded = extended(conv_in, (("seq", 0),), taps // 2)
    conv = jnp.zeros(stream.shape, jnp.float32)
    for offset in range(taps):
        conv = conv + padded[offset : offset + frames].astype(jnp.float32) * kernel[offset]
    return ((stream + jax.nn.silu(conv)) * valid[:, None]).astype(jnp.bfloat16)


def place_row(buffer, value, index):
    inside = (index >= 0) & (index < buffer.shape[0])
    clipped = jnp.clip(index, 0, buffer.shape[0] - 1)
    previous = lax.dynamic_index_in_dim(buffer, clipped, 0, keepdims=True)
    return lax.dynamic_update_index_in_dim(
        buffer, jnp.where(inside, value[None], previous), clipped, 0
    )


def shards(mel, lengths, stem_weight, w_qkv, w_out, norm_gains, conv_kernel):
    sections = lax.axis_size("section")
    section_index = lax.axis_index("section")
    seq_index = lax.axis_index("seq")
    micro = mel.shape[0]
    frames = mel.shape[1] // STRIDE
    full_stem, full_qkv, full_out = (
        lax.all_gather(stem_weight, ("seq", "dp"), axis=0, tiled=True),
        lax.all_gather(w_qkv, ("seq", "dp"), axis=1, tiled=True),
        lax.all_gather(w_out, ("seq", "dp"), axis=1, tiled=True),
    )
    full_qkv = full_qkv[0]
    full_out = full_out[0]
    gains = norm_gains[0]
    kernel = conv_kernel[0]
    model_width = full_out.shape[1]
    first_query = seq_index * frames
    positions = first_query + jnp.arange(frames, dtype=jnp.int32)
    valid_all = (positions[None, :] < lengths[:, None]).astype(jnp.float32)
    ticks = micro + sections - 1

    def tick(tick_index, carry):
        held_input, arrived, finished = carry
        micro_now = tick_index - section_index
        micro_slot = jnp.clip(micro_now, 0, micro - 1)
        valid = lax.dynamic_index_in_dim(valid_all, micro_slot, 0, keepdims=False)
        length = lax.dynamic_index_in_dim(lengths, micro_slot, 0, keepdims=False)

        def from_stem(operands):
            slot, mask, unused = operands
            grouped = lax.dynamic_index_in_dim(mel, slot, 0, keepdims=False).reshape(
                frames, STRIDE * mel.shape[2]
            )
            stem_out = (
                jax.nn.silu(jnp.dot(grouped, full_stem, preferred_element_type=jnp.float32))
                * mask[:, None]
            )
            return stem_out.astype(jnp.bfloat16)

        def from_before(operands):
            return operands[2]

        layer_input = lax.cond(
            section_index == 0, from_stem, from_before, (micro_slot, valid, held_input)
        )
        output = apply_layer(
            layer_input, valid, length, first_query, full_qkv, full_out, gains, kernel
        )
        received = from_behind(output, "section", 1)
        arriving = jnp.where(
            section_index == 0, tick_index - sections + 1, tick_index - section_index + 1
        )
        arrived = place_row(arrived, received, arriving)
        return (received, arrived, finished)

    start_input = jnp.zeros((frames, model_width), jnp.bfloat16)
    start_rows = jnp.zeros((micro, frames, model_width), jnp.bfloat16)
    held_input, arrived, finished = lax.fori_loop(
        0, ticks, tick, (start_input, start_rows, start_rows)
    )
    return arrived[None]


def solution(mesh):
    return jax.shard_map(
        shards,
        mesh=mesh,
        in_specs=(
            P("dp", "seq", None),
            P("dp"),
            P(("seq", "dp"), None),
            P("section", ("seq", "dp"), None),
            P("section", ("seq", "dp"), None),
            P("section", None, None),
            P("section", None, None),
        ),
        out_specs=P("section", "dp", "seq", None),
        check_vma=False,
    )
```

profile of v0, /device:TPU:1, one launch (start us, length us, event | category | flops | bytes accessed | tf_op | source)
XLA Modules:
  0.0 296.3 jit_solution(3266820856452127831)
XLA Ops:
  10.2 41.6 %all-gather.4.cloned.1.call-done = bf16[512,1536]{1,0:T(8,128)(2,1)} async-done(((bf16[32,1536]{1,0:T(8,128)(2,1)}), bf16[512,1536]{1,0:T(8,128)(2,1)}) %all-gather.4.cloned.1.call-update) | async-done | bytes 1572880 | tf_op jit(solution)/shard_map/all_gather | solution.py:100
  51.9 43.5 %all-gather.8.cloned.1.call-done = bf16[1,768,1536]{2,1,0:T(8,128)(2,1)} async-done(((bf16[1,48,1536]{2,1,0:T(8,128)(2,1)}), bf16[1,768,1536]{2,1,0:T(8,128)(2,1)}) %all-gather.8.cloned.1.call-update) | async-done | bytes 2359312 | tf_op jit(solution)/shard_map/all_gather | solution.py:102
  95.4 67.7 %all-gather.6.cloned.1.call-done = bf16[1,1536,2304]{2,1,0:T(8,128)(2,1)} async-done(((bf16[1,96,2304]{2,1,0:T(8,128)(2,1)}), bf16[1,1536,2304]{2,1,0:T(8,128)(2,1)}) %all-gather.6.cloned.1.call-update) | async-done | bytes 7077904 | tf_op jit(solution)/shard_map/all_gather | solution.py:101
  164.1 125.6 %while.23 = (s32[]{:T(128)}, bf16[128,1536]{1,0:T(8,128)(2,1)S(1)}, bf16[2,128,1536]{2,1,0:T(8,128)(2,1)}, pred[]{:T(512)}, s32[]{:T(128)}, /*index=5*/f32[2,128...) while((s32[]{:T(128)}, bf16[128,1536]{1,0:T(8,128)(2,1)S(1)}, ...), condition=%wide.region_10.11_spmd, body=%wide.region_0.10_spmd.sunk | while | flops 1578371712 | bytes 55258044 | solution.py:150
  164.1 2.1 conditional.2
  164.3 1.9 fusion.15
  166.5 4.2 %convolution_convert_fusion.4 = bf16[128,2304]{1,0:T(8,128)(2,1)S(1)} fusion(bf16[1536,2304]{1,0:T(8,128)(2,1)} %get-tuple-element.713, f32[128,1536]{1,0:T(8,128)S(1)} %get-tuple-element.645, f32[1536]{0:T(1024)S(1)} %get-tuple-element.646, f32[128]{0:T(128)S(1)} %add_rsqrt_fusion.4, f32[128]{0:T(128)S(1)} %broadcast_multiply_fusion.4), kind=kOutput, calls=%fused_computation.4.clone.1 | convolution fusion | flops 907051008 | bytes 8461312 | tf_op jit(solution)/shard_map/while/body/eval_jaxpr/dot_general | solution.py:71
  170.7 2.2 collective-permute-start
  172.9 3.4 %collective-permute-start.1 = (bf16[128,1536]{1,0:T(8,128)(2,1)S(1)}, bf16[128,1536]{1,0:T(8,128)(2,1)S(1)}, u32[]{:S(2)}, u32[]{:S(2)}) collective-permute-start(bf16[128,1536]{1,0:T(8,128)(2,1)S(1)} %slice.284), channel_id=1, source_target_pairs={{0,2},{2,4},{4,6},{6,8},{8,10},{10,12},{12,14},{1,3},{3,5},{5,7},{... | collective-permute-start | bytes 1179656 | tf_op jit(solution)/shard_map/while/body/eval_jaxpr/ppermute | solution.py:19
  177.9 1.9 collective-permute-done
  183.7 2.1 convolution_convert_fusion.5
  187.0 1.9 collective-permute-start.2
  188.9 4.4 %collective-permute-start.3 = (bf16[2,1536]{1,0:T(2,128)(2,1)S(1)}, bf16[2,1536]{1,0:T(2,128)(2,1)S(1)}, u32[]{:S(2)}, u32[]{:S(2)}) collective-permute-start(bf16[2,1536]{1,0:T(2,128)(2,1)S(1)} %get-tuple-element.656), channel_id=1, source_target_pairs={{0,2},{2,4},{4,6},{6,8},{8,10},{10,12},{12,14},{1,3},{3,5},{5,7},{... | collective-permute-start | bytes 18440 | tf_op jit(solution)/shard_map/while/body/eval_jaxpr/ppermute | solution.py:19
  194.9 9.3 %collective-permute-done.4 = bf16[128,1536]{1,0:T(8,128)(2,1)S(1)} collective-permute-done((bf16[128,1536]{1,0:T(8,128)(2,1)S(1)}, bf16[128,1536]{1,0:T(8,128)(2,1)S(1)}, u32[]{:S(2)}, u32[]{:S(2)}) %collective-permute-start.4) | collective-permute-done | bytes 393248 | tf_op jit(solution)/shard_map/while/body/eval_jaxpr/ppermute | solution.py:30
  205.2 2.1 conditional.2
  205.3 1.9 fusion.15
  207.6 4.2 %convolution_convert_fusion.4 = bf16[128,2304]{1,0:T(8,128)(2,1)S(1)} fusion(bf16[1536,2304]{1,0:T(8,128)(2,1)} %get-tuple-element.713, f32[128,1536]{1,0:T(8,128)S(1)} %get-tuple-element.645, f32[1536]{0:T(1024)S(1)} %get-tuple-element.646, f32[128]{0:T(128)S(1)} %add_rsqrt_fusion.4, f32[128]{0:T(128)S(1)} %broadcast_multiply_fusion.4), kind=kOutput, calls=%fused_computation.4.clone.1 | convolution fusion | flops 907051008 | bytes 8461312 | tf_op jit(solution)/shard_map/while/body/eval_jaxpr/dot_general | solution.py:71
  211.8 1.9 collective-permute-start
  213.7 5.0 %collective-permute-start.1 = (bf16[128,1536]{1,0:T(8,128)(2,1)S(1)}, bf16[128,1536]{1,0:T(8,128)(2,1)S(1)}, u32[]{:S(2)}, u32[]{:S(2)}) collective-permute-start(bf16[128,1536]{1,0:T(8,128)(2,1)S(1)} %slice.284), channel_id=1, source_target_pairs={{0,2},{2,4},{4,6},{6,8},{8,10},{10,12},{12,14},{1,3},{3,5},{5,7},{... | collective-permute-start | bytes 1179656 | tf_op jit(solution)/shard_map/while/body/eval_jaxpr/ppermute | solution.py:19
  220.3 1.9 collective-permute-done
  226.0 2.1 convolution_convert_fusion.5
  229.4 1.9 collective-permute-start.2
  231.3 4.4 %collective-permute-start.3 = (bf16[2,1536]{1,0:T(2,128)(2,1)S(1)}, bf16[2,1536]{1,0:T(2,128)(2,1)S(1)}, u32[]{:S(2)}, u32[]{:S(2)}) collective-permute-start(bf16[2,1536]{1,0:T(2,128)(2,1)S(1)} %get-tuple-element.656), channel_id=1, source_target_pairs={{0,2},{2,4},{4,6},{6,8},{8,10},{10,12},{12,14},{1,3},{3,5},{5,7},{... | collective-permute-start | bytes 18440 | tf_op jit(solution)/shard_map/while/body/eval_jaxpr/ppermute | solution.py:19
  237.2 9.3 %collective-permute-done.4 = bf16[128,1536]{1,0:T(8,128)(2,1)S(1)} collective-permute-done((bf16[128,1536]{1,0:T(8,128)(2,1)S(1)}, bf16[128,1536]{1,0:T(8,128)(2,1)S(1)}, u32[]{:S(2)}, u32[]{:S(2)}) %collective-permute-start.4) | collective-permute-done | bytes 393248 | tf_op jit(solution)/shard_map/while/body/eval_jaxpr/ppermute | solution.py:30
  247.6 2.1 conditional.2
  247.7 1.9 fusion.15
  249.9 4.2 %convolution_convert_fusion.4 = bf16[128,2304]{1,0:T(8,128)(2,1)S(1)} fusion(bf16[1536,2304]{1,0:T(8,128)(2,1)} %get-tuple-element.713, f32[128,1536]{1,0:T(8,128)S(1)} %get-tuple-element.645, f32[1536]{0:T(1024)S(1)} %get-tuple-element.646, f32[128]{0:T(128)S(1)} %add_rsqrt_fusion.4, f32[128]{0:T(128)S(1)} %broadcast_multiply_fusion.4), kind=kOutput, calls=%fused_computation.4.clone.1 | convolution fusion | flops 907051008 | bytes 8461312 | tf_op jit(solution)/shard_map/while/body/eval_jaxpr/dot_general | solution.py:71
  256.1 4.7 %collective-permute-start.1 = (bf16[128,1536]{1,0:T(8,128)(2,1)S(1)}, bf16[128,1536]{1,0:T(8,128)(2,1)S(1)}, u32[]{:S(2)}, u32[]{:S(2)}) collective-permute-start(bf16[128,1536]{1,0:T(8,128)(2,1)S(1)} %slice.284), channel_id=1, source_target_pairs={{0,2},{2,4},{4,6},{6,8},{8,10},{10,12},{12,14},{1,3},{3,5},{5,7},{... | collective-permute-start | bytes 1179656 | tf_op jit(solution)/shard_map/while/body/eval_jaxpr/ppermute | solution.py:19
  262.4 1.9 collective-permute-done
  268.2 2.1 convolution_convert_fusion.5
  273.4 4.4 %collective-permute-start.3 = (bf16[2,1536]{1,0:T(2,128)(2,1)S(1)}, bf16[2,1536]{1,0:T(2,128)(2,1)S(1)}, u32[]{:S(2)}, u32[]{:S(2)}) collective-permute-start(bf16[2,1536]{1,0:T(2,128)(2,1)S(1)} %get-tuple-element.656), channel_id=1, source_target_pairs={{0,2},{2,4},{4,6},{6,8},{8,10},{10,12},{12,14},{1,3},{3,5},{5,7},{... | collective-permute-start | bytes 18440 | tf_op jit(solution)/shard_map/while/body/eval_jaxpr/ppermute | solution.py:19
  279.4 9.3 %collective-permute-done.4 = bf16[128,1536]{1,0:T(8,128)(2,1)S(1)} collective-permute-done((bf16[128,1536]{1,0:T(8,128)(2,1)S(1)}, bf16[128,1536]{1,0:T(8,128)(2,1)S(1)}, u32[]{:S(2)}, u32[]{:S(2)}) %collective-permute-start.4) | collective-permute-done | bytes 393248 | tf_op jit(solution)/shard_map/while/body/eval_jaxpr/ppermute | solution.py:30
  (136 shorter events, 36.8 us)
Async XLA Ops:
  6.5 157.5 %copy-start.5 = (s32[2]{0:T(128)S(1)}, s32[2]{0:T(128)}, u32[]{:S(2)}) copy-start(s32[2]{0:T(128)} %param.12) | copy-start | bytes 28
  6.5 157.5 %copy-start.4 = (f32[1,2,1536]{2,1,0:T(2,128)S(1)}, f32[1,2,1536]{2,1,0:T(2,128)}, u32[]{:S(2)}) copy-start(f32[1,2,1536]{2,1,0:T(2,128)} %param.16) | copy-start | bytes 36868
  6.5 157.5 %copy-start.3 = (bf16[2,512,128]{2,1,0:T(8,128)(2,1)S(1)}, bf16[2,512,128]{2,1,0:T(8,128)(2,1)}, u32[]{:S(2)}) copy-start(bf16[2,512,128]{2,1,0:T(8,128)(2,1)} %param.11) | copy-start | bytes 786436
  6.5 45.4 %all-gather.4.cloned.1.call-start = ((), (), s32[]{:S(2)}) async-start(), calls=%async_computation | async-start | bytes 1671168 | tf_op jit(solution)/shard_map/all_gather | solution.py:100
  7.3 88.1 %all-gather.8.cloned.1.call-start = ((), (), s32[]{:S(2)}) async-start(), calls=%async_computation.2 | async-start | bytes 2506752 | tf_op jit(solution)/shard_map/all_gather | solution.py:102
  8.0 155.1 %all-gather.6.cloned.1.call-start = ((), (), s32[]{:S(2)}) async-start(), calls=%async_computation.1 | async-start | bytes 7520256 | tf_op jit(solution)/shard_map/all_gather | solution.py:101
  170.7 9.1 %collective-permute-start = (bf16[128,1536]{1,0:T(8,128)(2,1)S(1)}, bf16[128,1536]{1,0:T(8,128)(2,1)S(1)}, u32[]{:S(2)}, u32[]{:S(2)}) collective-permute-start(bf16[128,1536]{1,0:T(8,128)(2,1)S(1)} %slice.284), channel_id=1, source_target_pairs={{2,0},{4,2},{6,4},{8,6},{10,8},{12,10},{14,12},{3,1},{5,3},{7,5},{... | collective-permute-start | bytes 1179656 | tf_op jit(solution)/shard_map/while/body/eval_jaxpr/ppermute | solution.py:22
  172.9 8.1 %collective-permute-start.1 = (bf16[128,1536]{1,0:T(8,128)(2,1)S(1)}, bf16[128,1536]{1,0:T(8,128)(2,1)S(1)}, u32[]{:S(2)}, u32[]{:S(2)}) collective-permute-start(bf16[128,1536]{1,0:T(8,128)(2,1)S(1)} %slice.284), channel_id=1, source_target_pairs={{0,2},{2,4},{4,6},{6,8},{8,10},{10,12},{12,14},{1,3},{3,5},{5,7},{... | collective-permute-start | bytes 1179656 | tf_op jit(solution)/shard_map/while/body/eval_jaxpr/ppermute | solution.py:19
  183.7 2.1 copy-start
  186.6 17.6 %copy-start.1 = (bf16[2,128,1536]{2,1,0:T(8,128)(2,1)S(1)}, bf16[2,128,1536]{2,1,0:T(8,128)(2,1)}, u32[]{:S(2)}) copy-start(bf16[2,128,1536]{2,1,0:T(8,128)(2,1)} %get-tuple-element.687) | copy-start | bytes 2359300 | tf_op jit(solution)/shard_map/while
  187.0 6.4 %collective-permute-start.2 = (bf16[2,1536]{1,0:T(2,128)(2,1)S(1)}, bf16[2,1536]{1,0:T(2,128)(2,1)S(1)}, u32[]{:S(2)}, u32[]{:S(2)}) collective-permute-start(bf16[2,1536]{1,0:T(2,128)(2,1)S(1)} %get-tuple-element.655), channel_id=1, source_target_pairs={{2,0},{4,2},{6,4},{8,6},{10,8},{12,10},{14,12},{3,1},{5,3},{7,5},{... | collective-permute-start | bytes 18440 | tf_op jit(solution)/shard_map/while/body/eval_jaxpr/ppermute | solution.py:22
  188.9 5.1 %collective-permute-start.3 = (bf16[2,1536]{1,0:T(2,128)(2,1)S(1)}, bf16[2,1536]{1,0:T(2,128)(2,1)S(1)}, u32[]{:S(2)}, u32[]{:S(2)}) collective-permute-start(bf16[2,1536]{1,0:T(2,128)(2,1)S(1)} %get-tuple-element.656), channel_id=1, source_target_pairs={{0,2},{2,4},{4,6},{6,8},{8,10},{10,12},{12,14},{1,3},{3,5},{5,7},{... | collective-permute-start | bytes 18440 | tf_op jit(solution)/shard_map/while/body/eval_jaxpr/ppermute | solution.py:19
  194.8 9.4 %collective-permute-start.4 = (bf16[128,1536]{1,0:T(8,128)(2,1)S(1)}, bf16[128,1536]{1,0:T(8,128)(2,1)S(1)}, u32[]{:S(2)}, u32[]{:S(2)}) collective-permute-start(bf16[128,1536]{1,0:T(8,128)(2,1)S(1)} %multiply_convert_fusion.10), channel_id=1, source_target_pairs={{0,16},{16,0},{1,17},{17,1},{2,18},{18,2},{3,19},{19,3},{4,20},{20... | collective-permute-start | bytes 1179656 | tf_op jit(solution)/shard_map/while/body/eval_jaxpr/ppermute | solution.py:30
  204.3 0.9 copy-start.2
  211.8 10.4 %collective-permute-start = (bf16[128,1536]{1,0:T(8,128)(2,1)S(1)}, bf16[128,1536]{1,0:T(8,128)(2,1)S(1)}, u32[]{:S(2)}, u32[]{:S(2)}) collective-permute-start(bf16[128,1536]{1,0:T(8,128)(2,1)S(1)} %slice.284), channel_id=1, source_target_pairs={{2,0},{4,2},{6,4},{8,6},{10,8},{12,10},{14,12},{3,1},{5,3},{7,5},{... | collective-permute-start | bytes 1179656 | tf_op jit(solution)/shard_map/while/body/eval_jaxpr/ppermute | solution.py:22
  213.7 9.7 %collective-permute-start.1 = (bf16[128,1536]{1,0:T(8,128)(2,1)S(1)}, bf16[128,1536]{1,0:T(8,128)(2,1)S(1)}, u32[]{:S(2)}, u32[]{:S(2)}) collective-permute-start(bf16[128,1536]{1,0:T(8,128)(2,1)S(1)} %slice.284), channel_id=1, source_target_pairs={{0,2},{2,4},{4,6},{6,8},{8,10},{10,12},{12,14},{1,3},{3,5},{5,7},{... | collective-permute-start | bytes 1179656 | tf_op jit(solution)/shard_map/while/body/eval_jaxpr/ppermute | solution.py:19
  226.0 2.1 copy-start
  229.0 17.6 %copy-start.1 = (bf16[2,128,1536]{2,1,0:T(8,128)(2,1)S(1)}, bf16[2,128,1536]{2,1,0:T(8,128)(2,1)}, u32[]{:S(2)}) copy-start(bf16[2,128,1536]{2,1,0:T(8,128)(2,1)} %get-tuple-element.687) | copy-start | bytes 2359300 | tf_op jit(solution)/shard_map/while
  229.4 6.4 %collective-permute-start.2 = (bf16[2,1536]{1,0:T(2,128)(2,1)S(1)}, bf16[2,1536]{1,0:T(2,128)(2,1)S(1)}, u32[]{:S(2)}, u32[]{:S(2)}) collective-permute-start(bf16[2,1536]{1,0:T(2,128)(2,1)S(1)} %get-tuple-element.655), channel_id=1, source_target_pairs={{2,0},{4,2},{6,4},{8,6},{10,8},{12,10},{14,12},{3,1},{5,3},{7,5},{... | collective-permute-start | bytes 18440 | tf_op jit(solution)/shard_map/while/body/eval_jaxpr/ppermute | solution.py:22
  231.3 5.1 %collective-permute-start.3 = (bf16[2,1536]{1,0:T(2,128)(2,1)S(1)}, bf16[2,1536]{1,0:T(2,128)(2,1)S(1)}, u32[]{:S(2)}, u32[]{:S(2)}) collective-permute-start(bf16[2,1536]{1,0:T(2,128)(2,1)S(1)} %get-tuple-element.656), channel_id=1, source_target_pairs={{0,2},{2,4},{4,6},{6,8},{8,10},{10,12},{12,14},{1,3},{3,5},{5,7},{... | collective-permute-start | bytes 18440 | tf_op jit(solution)/shard_map/while/body/eval_jaxpr/ppermute | solution.py:19
  237.1 9.4 %collective-permute-start.4 = (bf16[128,1536]{1,0:T(8,128)(2,1)S(1)}, bf16[128,1536]{1,0:T(8,128)(2,1)S(1)}, u32[]{:S(2)}, u32[]{:S(2)}) collective-permute-start(bf16[128,1536]{1,0:T(8,128)(2,1)S(1)} %multiply_convert_fusion.10), channel_id=1, source_target_pairs={{0,16},{16,0},{1,17},{17,1},{2,18},{18,2},{3,19},{19,3},{4,20},{20... | collective-permute-start | bytes 1179656 | tf_op jit(solution)/shard_map/while/body/eval_jaxpr/ppermute | solution.py:30
  246.7 0.9 copy-start.2
  254.2 10.2 %collective-permute-start = (bf16[128,1536]{1,0:T(8,128)(2,1)S(1)}, bf16[128,1536]{1,0:T(8,128)(2,1)S(1)}, u32[]{:S(2)}, u32[]{:S(2)}) collective-permute-start(bf16[128,1536]{1,0:T(8,128)(2,1)S(1)} %slice.284), channel_id=1, source_target_pairs={{2,0},{4,2},{6,4},{8,6},{10,8},{12,10},{14,12},{3,1},{5,3},{7,5},{... | collective-permute-start | bytes 1179656 | tf_op jit(solution)/shard_map/while/body/eval_jaxpr/ppermute | solution.py:22
  256.1 9.4 %collective-permute-start.1 = (bf16[128,1536]{1,0:T(8,128)(2,1)S(1)}, bf16[128,1536]{1,0:T(8,128)(2,1)S(1)}, u32[]{:S(2)}, u32[]{:S(2)}) collective-permute-start(bf16[128,1536]{1,0:T(8,128)(2,1)S(1)} %slice.284), channel_id=1, source_target_pairs={{0,2},{2,4},{4,6},{6,8},{8,10},{10,12},{12,14},{1,3},{3,5},{5,7},{... | collective-permute-start | bytes 1179656 | tf_op jit(solution)/shard_map/while/body/eval_jaxpr/ppermute | solution.py:19
  268.2 2.1 copy-start
  271.1 17.6 %copy-start.1 = (bf16[2,128,1536]{2,1,0:T(8,128)(2,1)S(1)}, bf16[2,128,1536]{2,1,0:T(8,128)(2,1)}, u32[]{:S(2)}) copy-start(bf16[2,128,1536]{2,1,0:T(8,128)(2,1)} %get-tuple-element.687) | copy-start | bytes 2359300 | tf_op jit(solution)/shard_map/while
  271.5 6.4 %collective-permute-start.2 = (bf16[2,1536]{1,0:T(2,128)(2,1)S(1)}, bf16[2,1536]{1,0:T(2,128)(2,1)S(1)}, u32[]{:S(2)}, u32[]{:S(2)}) collective-permute-start(bf16[2,1536]{1,0:T(2,128)(2,1)S(1)} %get-tuple-element.655), channel_id=1, source_target_pairs={{2,0},{4,2},{6,4},{8,6},{10,8},{12,10},{14,12},{3,1},{5,3},{7,5},{... | collective-permute-start | bytes 18440 | tf_op jit(solution)/shard_map/while/body/eval_jaxpr/ppermute | solution.py:22
  273.4 5.1 %collective-permute-start.3 = (bf16[2,1536]{1,0:T(2,128)(2,1)S(1)}, bf16[2,1536]{1,0:T(2,128)(2,1)S(1)}, u32[]{:S(2)}, u32[]{:S(2)}) collective-permute-start(bf16[2,1536]{1,0:T(2,128)(2,1)S(1)} %get-tuple-element.656), channel_id=1, source_target_pairs={{0,2},{2,4},{4,6},{6,8},{8,10},{10,12},{12,14},{1,3},{3,5},{5,7},{... | collective-permute-start | bytes 18440 | tf_op jit(solution)/shard_map/while/body/eval_jaxpr/ppermute | solution.py:19
  279.3 9.4 %collective-permute-start.4 = (bf16[128,1536]{1,0:T(8,128)(2,1)S(1)}, bf16[128,1536]{1,0:T(8,128)(2,1)S(1)}, u32[]{:S(2)}, u32[]{:S(2)}) collective-permute-start(bf16[128,1536]{1,0:T(8,128)(2,1)S(1)} %multiply_convert_fusion.10), channel_id=1, source_target_pairs={{0,16},{16,0},{1,17},{17,1},{2,18},{18,2},{3,19},{19,3},{4,20},{20... | collective-permute-start | bytes 1179656 | tf_op jit(solution)/shard_map/while/body/eval_jaxpr/ppermute | solution.py:30
  288.8 0.9 copy-start.2
Sparse Core Ops, SparseCore 0:
  9.6 42.2 all-gather.3
  54.2 41.1 all-gather.7
  97.6 65.4 all-gather.5
where the time goes:
time: 297 us; the launch traced here: 296 us
  waiting for transfers between devices  194 us (65%)
  starting transfers between devices  38.3 us (13%)
  matrix products  32 us (11%)
  between operations  13.1 us (4%)
  local copies, waits for them, and re-layouts  9.66 us (3%)
  other arithmetic  8.08 us (3%)
    all_gather x1, waiting for transfers between devices, shards(): lax.all_gather(w_qkv, ('seq', 'dp'), axis=1, tiled=True)  67.7 us
    all_gather x1, waiting for transfers between devices, shards(): lax.all_gather(w_out, ('seq', 'dp'), axis=1, tiled=True)  43.5 us
    all_gather x1, waiting for transfers between devices, shards(): lax.all_gather(stem_weight, ('seq', 'dp'), axis=0, tiled=True)  41.6 us
    ppermute x3, waiting for transfers between devices, from_behind(): return lax.ppermute(value, axis, pairs)  28 us
    ppermute x6, starting transfers between devices, extended(): lax.ppermute(lax.slice_in_dim(block, block.shape[dim] - width, None, axis...  26.2 us
    dot_general x3, matrix products, apply_layer(): jnp.dot(normed, full_qkv, preferred_element_type=jnp.float32)  12.6 us
    ppermute x6, starting transfers between devices, extended(): lax.ppermute(lax.slice_in_dim(block, 0, width, axis=dim), axis, backward)  11.8 us
    dot_general x3, matrix products, band_attention(): jnp.einsum('hqk,khd->qhd', probs, value_rows, preferred_element_type=jnp....  6.32 us
  transfers between devices with their start and end apart: 18, of which 15 were waited for; matrix products, arithmetic and copies ran while one was open for 2% of the time, Pallas kernels for 0%

commit v1 on v0

v1 whole, which is shorter than its diff:
```python
import functools

import jax
import jax.numpy as jnp
from jax import lax
from jax.experimental import pallas as pl
from jax.experimental.pallas import tpu as pltpu
from jax.sharding import PartitionSpec as P

HEADS = 8
STRIDE = 4
RIM = 8
EDGE = 8
MARGIN = 16
PARTS = 4
LOG2E = 1.4426950408889634
MIB = 1024 * 1024


eps = 1e-05
masked_score = -1e30


def from_behind(value, axis, steps):
    count = lax.axis_size(axis)
    pairs = [(source, (source + steps) % count) for source in range(count)]
    return lax.ppermute(value, axis, pairs)


def from_seq(value, steps):
    count = lax.axis_size("seq")
    pairs = [(source, source + steps) for source in range(count) if 0 <= source + steps < count]
    return lax.ppermute(value, "seq", pairs)


def ring_gather(shard, place, beside):
    count, wide = lax.axis_size("seq"), lax.axis_size("dp")
    deep = count // 2
    chips = deep * wide
    order = [(z, x) for x in range(wide) for z in (range(deep) if x % 2 == 0 else reversed(range(deep)))]

    def flat(position, core):
        z, x = order[position % chips]
        return (2 * z + core) * wide + x

    around = [(flat(p, 0), flat(p + 1, 0)) for p in range(chips)]
    around += [(flat(p, 1), flat(p - 1, 1)) for p in range(chips)]
    swap = [(i, i ^ 1) for i in range(count)]
    partner = lax.ppermute(shard, "seq", swap)
    chains = [shard, partner]
    blocks = [[shard, partner]]
    placed, chosen = (), 0
    beside = list(beside)
    arrived = beside.pop(0)((), partner)
    for step in range(1, chips // 2 + 1):
        last = step == chips // 2
        if step > 2:
            chains[0], *ready = lax.optimization_barrier((chains[0], *blocks.pop(0)))
            placed = place(ready, chosen, placed)
            chosen += len(ready)
        if step == 2 and not last:
            chains[1], *arrived = lax.optimization_barrier((chains[1], *arrived))
        if last:
            chains[0], *held = lax.optimization_barrier((chains[0], *placed, *arrived))
            placed, arrived = held[: len(placed)], held[len(placed) :]
            for send in beside:
                arrived = send(arrived, chains[0])
        came = []
        for which in range(1 if last else 2):
            chains[which] = lax.ppermute(chains[which], ("seq", "dp"), around)
            if last:
                chains[which], *arrived = lax.optimization_barrier((chains[which], *arrived))
            came += [chains[which], lax.ppermute(chains[which], "seq", swap)]
        if step == 1:
            blocks[0] += came
        else:
            blocks.append(came)
    for ready in blocks:
        placed = place(ready, chosen, placed)
        chosen += len(ready)
    return placed, arrived


def ring_owners(count, wide):
    deep = count // 2
    chips = deep * wide
    seq_index, dp_index = lax.axis_index("seq"), lax.axis_index("dp")
    core = lax.rem(seq_index, 2)
    z = lax.div(seq_index, 2)
    position = deep * dp_index + jnp.where(lax.rem(dp_index, 2) == 0, z, deep - 1 - z)

    def owner(steps, which):
        at = lax.rem(position + steps + chips, chips)
        x = lax.div(at, deep)
        z = lax.rem(at, deep)
        z = jnp.where(lax.rem(x, 2) == 0, z, deep - 1 - z)
        return (2 * z + which) * wide + x

    toward = 2 * core - 1
    owners = [owner(0, core), owner(0, 1 - core)]
    for step in range(1, chips // 2 + 1):
        owners += [owner(toward * step, core), owner(-toward * step, 1 - core)]
        if step < chips // 2:
            owners += [owner(toward * step, 1 - core), owner(-toward * step, core)]
    return owners


def silu(value):
    half = 0.5 * value
    return half + half * jnp.tanh(half)


def normalized(value, gain):
    average = jnp.mean(value, axis=-1, keepdims=True)
    centered = value - average
    variance = jnp.mean(centered * centered, axis=-1, keepdims=True)
    return centered * lax.rsqrt(variance + eps) * gain


def cut_kernel(stem_ref, qkv_ref, out_ref, shard_ref, sems):
    width = shard_ref.shape[1]
    row, copies = 0, []
    for ref in (qkv_ref, out_ref, stem_ref):
        rows = ref.shape[0]
        for part in range(ref.shape[1] // width):
            copy = pltpu.make_async_copy(
                ref.at[:, pl.ds(part * width, width)],
                shard_ref.at[pl.ds(row, rows), :],
                sems.at[len(copies)],
            )
            copy.start()
            copies.append(copy)
            row += rows
    for copy in copies:
        copy.wait()


def cut_shard(stem, qkv, out):
    width = qkv.shape[1] // 3
    rows = 3 * qkv.shape[0] + 2 * out.shape[0] + 2 * stem.shape[0]
    return pl.pallas_call(
        cut_kernel,
        out_shape=jax.ShapeDtypeStruct((rows, width), jnp.bfloat16),
        in_specs=[pl.BlockSpec(memory_space=pl.ANY)] * 3,
        out_specs=pl.BlockSpec(memory_space=pltpu.VMEM),
        scratch_shapes=[pltpu.SemaphoreType.DMA((7,))],
        compiler_params=pltpu.CompilerParams(vmem_limit_bytes=56 * MIB),
    )(stem, qkv, out)


def place_kernel(*refs, blocks, chosen, count, wide, held):
    pieces, targets = refs[:blocks], refs[blocks + held :]
    owners = ring_owners(count, wide)[chosen : chosen + blocks]
    for piece, owner in zip(pieces, owners):
        row = 0
        for target in targets:
            rows = target.shape[1] // (count * wide)
            at = pl.multiple_of(owner * rows, rows)
            for part in range(target.shape[0]):
                target[part, pl.ds(at, rows), :] = piece[row : row + rows, :]
                row += rows


def place_blocks(pieces, chosen, shapes, held=()):
    vmem = pl.BlockSpec(memory_space=pltpu.VMEM)
    return pl.pallas_call(
        functools.partial(
            place_kernel,
            blocks=len(pieces),
            chosen=chosen,
            count=lax.axis_size("seq"),
            wide=lax.axis_size("dp"),
            held=len(held),
        ),
        out_shape=[jax.ShapeDtypeStruct(shape, jnp.bfloat16) for shape in shapes],
        in_specs=[vmem] * (len(pieces) + len(held)),
        out_specs=[vmem] * len(shapes),
        input_output_aliases={len(pieces) + i: i for i in range(len(held))},
        compiler_params=pltpu.CompilerParams(vmem_limit_bytes=4 * MIB),
    )(*pieces, *held)


def group_kernel(lengths_ref, own_ref, partner_ref, got_ref, far_ref, grouped_ref, kept_ref, raw):
    span, taken = grouped_ref.shape[1], raw.shape[1]
    rows, edge = own_ref.shape[1], far_ref.shape[1]
    core = lax.rem(lax.axis_index("seq"), 2)
    low, high = edge + rows, edge + 2 * rows
    for slot in range(grouped_ref.shape[0]):
        kept_ref[slot] = lengths_ref[slot]

        def put(start, ref, at, size):
            raw[start : start + size, :] = ref[slot, at : at + size, :].astype(jnp.float32)

        put(low, own_ref, 0, rows)

        @pl.when(core == 0)
        def _():
            put(0, got_ref, 0, low)
            put(high, partner_ref, 0, rows)
            put(high + rows, far_ref, 0, edge)

        @pl.when(core == 1)
        def _():
            put(0, far_ref, 0, edge)
            put(edge, partner_ref, 0, rows)
            put(high, got_ref, edge, rows)
            put(high + rows, got_ref, 0, edge)

        for step in range(STRIDE):
            grouped_ref[slot, :, step * taken : (step + 1) * taken] = raw[
                pl.ds(step, span, stride=STRIDE), :
            ].astype(jnp.bfloat16)


def group_rows(lengths, own, partner, got, far):
    micro, rows, taken = own.shape
    raw = 3 * rows + 2 * far.shape[1]
    vmem = pl.BlockSpec(memory_space=pltpu.VMEM)
    smem = pl.BlockSpec(memory_space=pltpu.SMEM)
    return pl.pallas_call(
        group_kernel,
        out_shape=[
            jax.ShapeDtypeStruct((micro, raw // STRIDE, STRIDE * taken), own.dtype),
            jax.ShapeDtypeStruct(lengths.shape, lengths.dtype),
        ],
        in_specs=[smem] + [vmem] * 4,
        out_specs=[vmem, smem],
        scratch_shapes=[pltpu.VMEM((raw, taken), jnp.float32)],
        compiler_params=pltpu.CompilerParams(vmem_limit_bytes=4 * MIB),
    )(lengths, own, partner, got, far)


def stem_kernel(lengths_ref, grouped_ref, weight_ref, result_ref, *, slot, frames):
    span, width = grouped_ref.shape[1], weight_ref.shape[2]
    first = lax.axis_index("seq") * frames - (span - frames) // 2
    positions = first + lax.broadcasted_iota(jnp.int32, (span, 1), 0)
    valid = ((positions >= 0) & (positions < lengths_ref[slot])).astype(jnp.float32)
    for half in range(weight_ref.shape[0]):
        value = jnp.dot(grouped_ref[slot], weight_ref[half], preferred_element_type=jnp.float32)
        value = silu(value) * valid
        result_ref[:, half * width : (half + 1) * width] = value.astype(jnp.bfloat16)


def apply_stem(grouped, slot, lengths, frames, weight):
    vmem = pl.BlockSpec(memory_space=pltpu.VMEM)
    shape = (grouped.shape[1], weight.shape[0] * weight.shape[2])
    return pl.pallas_call(
        functools.partial(stem_kernel, slot=slot, frames=frames),
        out_shape=jax.ShapeDtypeStruct(shape, jnp.bfloat16),
        in_specs=[pl.BlockSpec(memory_space=pltpu.SMEM)] + [vmem] * 2,
        out_specs=vmem,
        compiler_params=pltpu.CompilerParams(vmem_limit_bytes=10 * MIB),
    )(lengths, grouped, weight)


def project(inputs, ranges, gains_ref, qkv_w, normed, queries, keys, values, middle, frames):
    model = qkv_w.shape[1]
    span, rows = normed.shape[0], queries.shape[0]
    width = middle.shape[0]
    shift = (width - rows) // 2
    row = (span - sum(end - at for at, end in ranges)) // 2
    if row > 0:
        for edge in (0, span - row):
            normed[edge : edge + row, :] = jnp.zeros((row, model), jnp.bfloat16)
    for ref, (at, end) in zip(inputs, ranges):
        while at < end:
            step = min(32, end - at) if row % 16 == 0 else min(8, end - at)
            taken = ref[at : at + step, :]
            normed[row : row + step, :] = normalized(
                taken.astype(jnp.float32), gains_ref[0:1, :]
            ).astype(jnp.bfloat16)
            low, high = max(row, frames), min(row + step, frames + width)
            if low < high:
                middle[low - frames : high - frames, :] = taken[low - row : high - row]
            row += step
            at += step
    for part, target in ((1, keys), (2, values)):
        target[...] = jnp.dot(
            normed[...], qkv_w[part], preferred_element_type=jnp.float32
        ).astype(jnp.bfloat16)
    asked = jnp.dot(
        normed[frames : frames + width, :], qkv_w[0], preferred_element_type=jnp.float32
    )
    queries[...] = asked[shift : shift + rows, :].astype(jnp.bfloat16)


def attend(
    queries, keys, values, middle, gains_ref, taps_ref, out_w, result_ref, context, stream, conv_in,
    first, length, frames, heads,
):
    width, model = out_w.shape[1], 2 * out_w.shape[2]
    head = width // heads
    rows, span = queries.shape[0], keys.shape[0]
    made = result_ref.shape[0]
    rim = (made - frames) // 2
    margin = (span - 3 * frames) // 2
    shift = (middle.shape[0] - rows) // 2
    column = 256
    query_pos = lax.broadcasted_iota(jnp.int32, (rows, span), 0) - rim - EDGE
    key_pos = lax.broadcasted_iota(jnp.int32, (rows, span), 1) - frames - margin
    allowed = (key_pos >= -first) & (key_pos < length - first)
    allowed = allowed & (jnp.abs(query_pos - key_pos) <= frames)
    bias = jnp.where(allowed, 0.0, masked_score)
    scale = LOG2E / head**0.5
    lane = lax.broadcasted_iota(jnp.int32, (rows, column), 1)

    def window_of(index):
        window = min(index * head // 128 * 128, width - column)
        low = index * head - window
        return pl.ds(window, column), (lane >= low) & (lane < low + head)

    def scores_of(index):
        cut, mine = window_of(index)
        query = queries[:, cut]
        query = jnp.where(mine, query, jnp.zeros_like(query))
        return lax.dot_general(
            query, keys[:, cut], (((1,), (1,)), ((), ())), preferred_element_type=jnp.float32
        )

    scores = scores_of(0)
    for index in range(heads):
        later = scores_of(index + 1) if index + 1 < heads else None
        cut, mine = window_of(index)
        scores = scores * scale + bias
        expon = jnp.exp2(scores - jnp.max(scores, axis=-1, keepdims=True))
        total = jnp.sum(expon, axis=-1, keepdims=True)
        mixed = jnp.dot(
            expon.astype(jnp.bfloat16), values[:, cut], preferred_element_type=jnp.float32
        ) * (1.0 / total)
        context[:, cut] = jnp.where(mine, mixed, context[:, cut])
        scores = later

    positions = first - rim - EDGE + lax.broadcasted_iota(jnp.int32, (rows, 1), 0)
    valid = ((positions >= 0) & (positions < length)).astype(jnp.float32)
    mixed = context[...].astype(jnp.bfloat16)
    for half in range(2):
        cut = pl.ds(half * width, width)
        stream[:, cut] = middle[:, cut].astype(jnp.float32)[shift : shift + rows] + jnp.dot(
            mixed, out_w[half], preferred_element_type=jnp.float32
        )

    for at in range(0, rows, 16):
        conv_in[at : at + 16, :] = (
            (normalized(stream[at : at + 16, :], gains_ref[1:2, :]) * valid[at : at + 16])
            .astype(jnp.bfloat16)
            .astype(jnp.float32)
        )

    taps = taps_ref.shape[0]
    for at in range(0, made, 16):
        conv = jnp.zeros((16, model), jnp.float32)
        for tap in range(taps):
            low = EDGE - taps // 2 + tap + at
            conv = conv + conv_in[low : low + 16, :] * taps_ref[tap : tap + 1, :]
        base = EDGE + at
        value = stream[base : base + 16, :] + silu(conv)
        result_ref[at : at + 16, :] = (value * valid[base : base + 16]).astype(jnp.bfloat16)


def layer_kernel(lengths_ref, *refs, slot, ranges, frames, heads):
    inputs, refs = refs[: len(ranges)], refs[len(ranges) :]
    gains_ref, taps_ref, qkv_w, out_w, result_ref = refs[:5]
    normed, queries, keys, values, middle, context, stream, conv_in = refs[5:]
    project(inputs, ranges, gains_ref, qkv_w, normed, queries, keys, values, middle, frames)
    attend(
        queries, keys, values, middle, gains_ref, taps_ref, out_w, result_ref, context, stream, conv_in,
        lax.axis_index("seq") * frames, lengths_ref[slot], frames, heads,
    )


def layer_buffers(frames, rim, model, width):
    span, rows, held = 3 * frames + 2 * MARGIN, frames + 2 * (rim + EDGE), frames + 2 * MARGIN
    return (
        [(span, model)],
        [(rows, width), (span, width), (span, width), (held, model)],
        [(rows, width), (rows, model), (rows, model)],
    )


def on_vmem(shapes, kind):
    return [pltpu.VMEM(shape, kind) for shape in shapes]


def apply_layer(segments, slot, lengths, frames, rim, weights, gains, kernel):
    segments, *ranges = zip(*segments)
    model, width = weights[0].shape[1:]
    normed, projected, scratch = layer_buffers(frames, rim, model, width)
    vmem = pl.BlockSpec(memory_space=pltpu.VMEM)
    body = functools.partial(
        layer_kernel, slot=slot, ranges=tuple(zip(*ranges)), frames=frames, heads=HEADS
    )
    return pl.pallas_call(
        body,
        out_shape=jax.ShapeDtypeStruct((frames + 2 * rim, model), jnp.bfloat16),
        in_specs=[pl.BlockSpec(memory_space=pltpu.SMEM)] + [vmem] * (len(segments) + 4),
        out_specs=vmem,
        scratch_shapes=on_vmem(normed + projected, jnp.bfloat16) + on_vmem(scratch, jnp.float32),
        compiler_params=pltpu.CompilerParams(vmem_limit_bytes=11 * MIB),
        cost_estimate=pl.CostEstimate(
            flops=8 * normed[0][0] * model * width + 4 * scratch[0][0] * normed[0][0] * width,
            bytes_accessed=8 * width * model,
            transcendentals=HEADS * scratch[0][0] * normed[0][0],
        ),
    )(lengths, *segments, gains, kernel, *weights)


def in_columns(weight, width):
    return jnp.stack(
        [weight[:, low : low + width] for low in range(0, weight.shape[1], width)]
    )


def gather_weights(stem, qkv, out, beside):
    devices = lax.axis_size("seq") * lax.axis_size("dp")
    width = qkv.shape[1] // 3
    if any(weight.shape[0] % 16 for weight in (stem, qkv, out)):
        whole = [lax.all_gather(w, ("seq", "dp"), axis=0, tiled=True) for w in (qkv, out, stem)]
        arrived = ()
        for send in beside:
            arrived = send(arrived, stem)
        return [in_columns(weight, width) for weight in whole], arrived
    shapes = [(w.shape[1] // width, w.shape[0] * devices, width) for w in (qkv, out, stem)]

    def place(blocks, chosen, weights):
        return place_blocks(blocks, chosen, shapes, weights)

    return ring_gather(cut_shard(stem, qkv, out), place, beside)


def edge_kernel(own_ref, partner_ref, message_ref):
    rows = own_ref.shape[1]
    edge = message_ref.shape[1] - rows
    core = lax.rem(lax.axis_index("seq"), 2)
    message_ref[:, edge:, :] = partner_ref[...]

    @pl.when(core == 0)
    def _():
        message_ref[:, :edge, :] = own_ref[:, rows - edge :, :]

    @pl.when(core == 1)
    def _():
        message_ref[:, :edge, :] = own_ref[:, :edge, :]


def far_kernel(got_ref, message_ref):
    edge = message_ref.shape[1]
    core = lax.rem(lax.axis_index("seq"), 2)

    @pl.when(core == 0)
    def _():
        message_ref[...] = got_ref[:, got_ref.shape[1] - edge :, :]

    @pl.when(core == 1)
    def _():
        message_ref[...] = got_ref[:, edge : 2 * edge, :]


def mel_beside(mel, lengths, edge):
    count = lax.axis_size("seq")
    micro, rows, taken = mel.shape
    swap = [(i, i ^ 1) for i in range(count)]
    away = [(i, i + 2) for i in range(0, count - 2, 2)] + [(i, i - 2) for i in range(3, count, 2)]

    def message(kernel, sources, size):
        vmem = pl.BlockSpec(memory_space=pltpu.VMEM)
        return pl.pallas_call(
            kernel,
            out_shape=jax.ShapeDtypeStruct((micro, size, taken), mel.dtype),
            in_specs=[vmem] * len(sources),
            out_specs=vmem,
            compiler_params=pltpu.CompilerParams(vmem_limit_bytes=4 * MIB),
        )(*sources)

    def send_near(_, after):
        own, _ = lax.optimization_barrier((mel, after))
        partner = lax.ppermute(own, "seq", swap)
        sent = message(edge_kernel, (own, partner), rows + edge)
        return own, partner, lax.ppermute(sent, "seq", away)

    def send_far(held, after):
        own, partner, got, _ = lax.optimization_barrier((*held, after))
        sent = message(far_kernel, (got,), edge)
        return group_rows(lengths, own, partner, got, lax.ppermute(sent, "seq", swap))

    return send_near, send_far


def beside_rows(rows, frames, rim, margin):
    count = frames + 2 * rim
    if rim == margin:
        return [
            (from_seq(rows, 1), 0, frames + rim),
            (rows, rim, rim + frames),
            (from_seq(rows, -1), rim, count),
        ]
    dim = rows.ndim - 2
    rows = lax.slice_in_dim(rows, rim, rim + frames, axis=dim)
    below = lax.slice_in_dim(rows, frames - margin, frames, axis=dim)
    above = lax.slice_in_dim(rows, 0, margin, axis=dim)
    return [
        (from_seq(below, 2), 0, margin),
        (from_seq(rows, 1), 0, frames),
        (rows, 0, frames),
        (from_seq(rows, -1), 0, frames),
        (from_seq(above, -2), 0, margin),
    ]


def arrive_kernel(*refs, slot, ranges):
    inputs, out_ref, sems = refs[: len(ranges)], refs[-2], refs[-1]
    sections = len(ranges)
    section = lax.axis_index("section")
    for tick, (ref, (low, high)) in enumerate(zip(inputs, ranges)):

        @pl.when(lax.rem(section + sections - 1, sections) == tick)
        def _():
            rows = (high - low) // PARTS
            copies = [
                pltpu.make_async_copy(
                    ref.at[pl.ds(low + part * rows, rows), :],
                    out_ref.at[0, slot, pl.ds(part * rows, rows), :],
                    sems.at[part],
                )
                for part in range(PARTS)
            ]
            for copy in copies:
                copy.start()
            for copy in copies:
                copy.wait()


def write_arrival(received, slot, micro, held):
    arrays, *ranges = zip(*received)
    ranges = tuple(zip(*ranges))
    shape = (1, micro, ranges[0][1] - ranges[0][0], arrays[0].shape[1])
    anywhere = pl.BlockSpec(memory_space=pl.ANY)
    return pl.pallas_call(
        functools.partial(arrive_kernel, slot=slot, ranges=ranges),
        out_shape=jax.ShapeDtypeStruct(shape, jnp.bfloat16),
        in_specs=[pl.BlockSpec(memory_space=pltpu.VMEM)] * len(arrays) + [anywhere] * len(held),
        out_specs=anywhere,
        input_output_aliases={len(arrays): 0} if held else {},
        scratch_shapes=[pltpu.SemaphoreType.DMA((PARTS,))],
        compiler_params=pltpu.CompilerParams(vmem_limit_bytes=4 * MIB),
    )(*arrays, *held)


def shards(mel, lengths, stem_weight, w_qkv, w_out, norm_gains, conv_kernel):
    sections = lax.axis_size("section")
    micro = mel.shape[0]
    frames = mel.shape[1] // STRIDE
    sends = mel_beside(mel, lengths, MARGIN * STRIDE)
    (*weights, full_stem), (grouped, lengths) = gather_weights(stem_weight, w_qkv[0], w_out[0], sends)
    gains = norm_gains[0]
    kernel = conv_kernel[0]
    received = [[] for _ in range(micro)]
    values = [None] * micro
    rim = RIM if sections > 1 else 0
    for slot in range(micro):
        if slot > 0:
            grouped, output = lax.optimization_barrier((grouped, output))
        stem = apply_stem(grouped, slot, lengths, frames, full_stem)
        segments = [(stem, 0, stem.shape[0])]
        output = apply_layer(segments, slot, lengths, frames, rim, weights, gains, kernel)
        values[slot] = from_behind(output, "section", 1)
        received[slot].append((values[slot], rim, rim + frames))
    for tick in range(1, sections):
        held = [beside_rows(value, frames, rim, RIM) for value in values]
        for slot in range(micro):
            output = apply_layer(held[slot], slot, lengths, frames, 0, weights, gains, kernel)
            values[slot] = from_behind(output, "section", 1)
            received[slot].append((values[slot], 0, frames))
        rim = 0
    arrived = ()
    for slot in range(micro):
        arrived = (write_arrival(received[slot], slot, micro, arrived),)
    return arrived[0]


def solution(mesh):
    return jax.shard_map(
        shards,
        mesh=mesh,
        in_specs=(
            P("dp", "seq", None),
            P("dp"),
            P(("seq", "dp"), None),
            P("section", ("seq", "dp"), None),
            P("section", ("seq", "dp"), None),
            P("section", None, None),
            P("section", None, None),
        ),
        out_specs=P("section", "dp", "seq", None),
        check_vma=False,
    )
```

time: 297 us -> 127 us (0.43)
  waiting for transfers between devices: 194 us -> 47.9 us
  Pallas kernels: 0 us -> 37.2 us
  matrix products: 32 us -> 0 us
  between operations: 13.1 us -> 0.41 us
  other arithmetic: 8.08 us -> 0 us
  local copies, waits for them, and re-layouts: 9.66 us -> 2.07 us
    all_gather x3 -> x0, waiting for transfers between devices: 153 us -> none  [the longest x1 67.7 us: shards(): lax.all_gather(w_qkv, ('seq', 'dp'), axis=1, tiled=True)]
    pallas_call x0 -> x16, Pallas kernels: none -> 37.2 us  [the longest x4 28 us: apply_layer(): pl.pallas_call(body, out_shape=jax.ShapeDtypeStruct((frames + 2 * rim, mo...]
    dot_general x12 -> x0, matrix products: 26.5 us -> none  [the longest x3 12.6 us: apply_layer(): jnp.dot(normed, full_qkv, preferred_element_type=jnp.float32)]
    ppermute x12 -> x22, waiting for transfers between devices: 11.3 us -> 36.8 us  [the longest x7 30.8 us: ring_gather(): chains[which] = lax.ppermute(chains[which], ('seq', 'dp'), around)]
    ppermute x3 -> x4, waiting for transfers between devices: 28 us -> 11 us  [from_behind(): return lax.ppermute(value, axis, pairs)]
    sub x3 -> x0, matrix products: 5.58 us -> none  [band_attention(): expon = jnp.exp(scores - highest)]
    convert_element_type x7 -> x0, other arithmetic: 3.72 us -> none  [the longest x3 2.07 us: apply_layer(): return ((stream + jax.nn.silu(conv)) * valid[:, None]).astype(jnp.bfloat16)]
    ppermute x12 -> x22, starting transfers between devices: 38 us -> 34.8 us  [the longest x4 14.5 us: from_seq(): return lax.ppermute(value, 'seq', pairs)]
  transfers between devices with their start and end apart: 18 -> 26, of which waited for: 15 -> 15; matrix products, arithmetic and copies ran while one was open for 2% -> 0% of each run, Pallas kernels for 0% -> 20%
where the time goes in v1:
time: 127 us; the launch traced here: 125 us
  waiting for transfers between devices  47.9 us (38%)
  starting transfers between devices  37.5 us (30%)
  Pallas kernels  37.2 us (29%)
  local copies, waits for them, and re-layouts  2.07 us (2%)
    ppermute x7, waiting for transfers between devices, ring_gather(): chains[which] = lax.ppermute(chains[which], ('seq', 'dp'), around)  30.8 us
    pallas_call x4, Pallas kernels, apply_layer(): pl.pallas_call(body, out_shape=jax.ShapeDtypeStruct((frames + 2 * rim, mo...  28 us
    ppermute x4, starting transfers between devices, from_seq(): return lax.ppermute(value, 'seq', pairs)  14.5 us
    ppermute x7, starting transfers between devices, ring_gather(): chains[which] = lax.ppermute(chains[which], ('seq', 'dp'), around)  13.1 us
    ppermute x4, waiting for transfers between devices, from_behind(): return lax.ppermute(value, axis, pairs)  11 us
    pallas_call x2, Pallas kernels, apply_stem(): pl.pallas_call(functools.partial(stem_kernel, slot=slot, frames=frames),...  3.1 us
    ppermute x7, starting transfers between devices, ring_gather(): came += [chains[which], lax.ppermute(chains[which], 'seq', swap)]  2.87 us
    ppermute x4, starting transfers between devices, from_behind(): return lax.ppermute(value, axis, pairs)  2.75 us
  transfers between devices with their start and end apart: 26, of which 15 were waited for; matrix products, arithmetic and copies ran while one was open for 0% of the time, Pallas kernels for 20%

profile of v1, /device:TPU:1, one launch (start us, length us, event | category | flops | bytes accessed | tf_op | source)
XLA Modules:
  0.0 125.0 jit_solution(4682273670180315215)
XLA Ops:
  0.0 2.0 %shard_map.73.refs_0_ = bf16[448,768]{1,0:T(8,128)(2,1)} custom-call(bf16[32,1536]{1,0:T(8,128)(2,1)} %stem_ref.1, bf16[96,2304]{1,0:T(8,128)(2,1)} %bitcast.14, bf16[48,1536]{1,0:T(8,128)(2,1)} %bitcast.15), custom_call_target="tpu_custom_call" | custom-call | tf_op jit(solution)/shard_map/pallas_call | solution.py:141
  2.2 2.7 %collective-permute-start = (bf16[448,768]{1,0:T(8,128)(2,1)}, bf16[448,768]{1,0:T(8,128)(2,1)S(1)}, u32[]{:S(2)}, u32[]{:S(2)}) collective-permute-start(bf16[448,768]{1,0:T(8,128)(2,1)} %shard_map.73.refs_0_), channel_id=1, source_target_pairs={{0,4},{4,8},{8,12},{12,13},{13,9},{9,5},{5,1},{1,0},{2,3},{6,2},{1... | collective-permute-start | bytes 2064392 | tf_op jit(solution)/shard_map/ppermute | solution.py:70
  4.8 2.0 %collective-permute-start.4 = (bf16[448,768]{1,0:T(8,128)(2,1)S(1)}, bf16[448,768]{1,0:T(8,128)(2,1)S(1)}, u32[]{:S(2)}, u32[]{:S(2)}) collective-permute-start(bf16[448,768]{1,0:T(8,128)(2,1)S(1)} %collective-permute-done.2.refs_1_), channel_id=1, source_target_pairs={{0,4},{4,8},{8,12},{12,13},{13,9},{9,5},{5,1},{1,0},{2,3},{6,2},{1... | collective-permute-start | bytes 2064392 | tf_op jit(solution)/shard_map/ppermute | solution.py:70
  7.6 1.4 %collective-permute-done.8.partner_ref = bf16[2,512,128]{2,1,0:T(8,128)(2,1)S(1)} collective-permute-done((bf16[2,512,128]{2,1,0:T(8,128)(2,1)}, bf16[2,512,128]{2,1,0:T(8,128)(2,1)S(1)}, u32[]{:S(2)}, u32[]{:S(2)}) %collective-permute-start.8) | collective-permute-done | bytes 262176 | tf_op jit(solution)/shard_map/ppermute | solution.py:476
  11.2 2.5 %collective-permute-done.refs_2_ = bf16[448,768]{1,0:T(8,128)(2,1)S(1)} collective-permute-done((bf16[448,768]{1,0:T(8,128)(2,1)}, bf16[448,768]{1,0:T(8,128)(2,1)S(1)}, u32[]{:S(2)}, u32[]{:S(2)}) %collective-permute-start) | collective-permute-done | bytes 688160 | tf_op jit(solution)/shard_map/ppermute | solution.py:70
  13.8 1.4 %collective-permute-start.1 = (bf16[448,768]{1,0:T(8,128)(2,1)S(1)}, bf16[448,768]{1,0:T(8,128)(2,1)S(1)}, u32[]{:S(2)}, u32[]{:S(2)}) collective-permute-start(bf16[448,768]{1,0:T(8,128)(2,1)S(1)} %collective-permute-done.refs_2_), channel_id=1, source_target_pairs={{0,4},{4,8},{8,12},{12,13},{13,9},{9,5},{5,1},{1,0},{2,3},{6,2},{1... | collective-permute-start | bytes 2064392 | tf_op jit(solution)/shard_map/ppermute | solution.py:70
  16.4 4.7 %collective-permute-done.4.refs_4_ = bf16[448,768]{1,0:T(8,128)(2,1)S(1)} collective-permute-done((bf16[448,768]{1,0:T(8,128)(2,1)S(1)}, bf16[448,768]{1,0:T(8,128)(2,1)S(1)}, u32[]{:S(2)}, u32[]{:S(2)}) %collective-permute-start.4) | collective-permute-done | bytes 688160 | tf_op jit(solution)/shard_map/ppermute | solution.py:70
  21.7 2.6 %collective-permute-done.9.got_ref = bf16[2,576,128]{2,1,0:T(8,128)(2,1)S(1)} collective-permute-done((bf16[2,576,128]{2,1,0:T(8,128)(2,1)S(1)}, bf16[2,576,128]{2,1,0:T(8,128)(2,1)S(1)}, u32[]{:S(2)}, u32[]{:S(2)}) %collective-permute-start.9) | collective-permute-done | bytes 294944 | tf_op jit(solution)/shard_map/ppermute | solution.py:478
  24.3 2.3 %collective-permute-start.10 = (bf16[448,768]{1,0:T(8,128)(2,1)S(1)}, bf16[448,768]{1,0:T(8,128)(2,1)S(1)}, u32[]{:S(2)}, u32[]{:S(2)}) collective-permute-start(bf16[448,768]{1,0:T(8,128)(2,1)S(1)} %collective-permute-done.4.refs_4_), channel_id=1, source_target_pairs={{0,4},{4,8},{8,12},{12,13},{13,9},{9,5},{5,1},{1,0},{2,3},{6,2},{1... | collective-permute-start | bytes 2064392 | tf_op jit(solution)/shard_map/ppermute | solution.py:70
  26.6 5.1 %collective-permute-done.1.refs_0_ = bf16[448,768]{1,0:T(8,128)(2,1)S(1)} collective-permute-done((bf16[448,768]{1,0:T(8,128)(2,1)S(1)}, bf16[448,768]{1,0:T(8,128)(2,1)S(1)}, u32[]{:S(2)}, u32[]{:S(2)}) %collective-permute-start.1) | collective-permute-done | bytes 688160 | tf_op jit(solution)/shard_map/ppermute | solution.py:70
  31.8 2.1 %collective-permute-start.6 = (bf16[448,768]{1,0:T(8,128)(2,1)S(1)}, bf16[448,768]{1,0:T(8,128)(2,1)S(1)}, u32[]{:S(2)}, u32[]{:S(2)}) collective-permute-start(bf16[448,768]{1,0:T(8,128)(2,1)S(1)} %collective-permute-done.1.refs_0_), channel_id=1, source_target_pairs={{0,4},{4,8},{8,12},{12,13},{13,9},{9,5},{5,1},{1,0},{2,3},{6,2},{1... | collective-permute-start | bytes 2064392 | tf_op jit(solution)/shard_map/ppermute | solution.py:70
  34.0 5.1 %collective-permute-done.10.refs_2_ = bf16[448,768]{1,0:T(8,128)(2,1)S(1)} collective-permute-done((bf16[448,768]{1,0:T(8,128)(2,1)S(1)}, bf16[448,768]{1,0:T(8,128)(2,1)S(1)}, u32[]{:S(2)}, u32[]{:S(2)}) %collective-permute-start.10) | collective-permute-done | bytes 688160 | tf_op jit(solution)/shard_map/ppermute | solution.py:70
  40.6 2.2 %collective-permute-start.16 = (bf16[448,768]{1,0:T(8,128)(2,1)S(1)}, bf16[448,768]{1,0:T(8,128)(2,1)S(1)}, u32[]{:S(2)}, u32[]{:S(2)}) collective-permute-start(bf16[448,768]{1,0:T(8,128)(2,1)S(1)} %collective-permute-done.10.refs_2_), channel_id=1, source_target_pairs={{0,4},{4,8},{8,12},{12,13},{13,9},{9,5},{5,1},{1,0},{2,3},{6,2},{1... | collective-permute-start | bytes 2064392 | tf_op jit(solution)/shard_map/ppermute | solution.py:70
  42.8 3.6 %collective-permute-done.6.refs_0_ = bf16[448,768]{1,0:T(8,128)(2,1)S(1)} collective-permute-done((bf16[448,768]{1,0:T(8,128)(2,1)S(1)}, bf16[448,768]{1,0:T(8,128)(2,1)S(1)}, u32[]{:S(2)}, u32[]{:S(2)}) %collective-permute-start.6) | collective-permute-done | bytes 688160 | tf_op jit(solution)/shard_map/ppermute | solution.py:70
  47.2 2.2 %collective-permute-start.13 = (bf16[2,64,128]{2,1,0:T(8,128)(2,1)S(1)}, bf16[2,64,128]{2,1,0:T(8,128)(2,1)S(1)}, u32[]{:S(2)}, u32[]{:S(2)}) collective-permute-start(bf16[2,64,128]{2,1,0:T(8,128)(2,1)S(1)} %shard_map.77), channel_id=1, source_target_pairs={{0,2},{2,0},{4,6},{6,4},{8,10},{10,8},{12,14},{14,12},{1,3},{3,1},... | collective-permute-start | bytes 98312 | tf_op jit(solution)/shard_map/ppermute | solution.py:483
  49.4 4.4 %collective-permute-done.16.refs_2_ = bf16[448,768]{1,0:T(8,128)(2,1)S(1)} collective-permute-done((bf16[448,768]{1,0:T(8,128)(2,1)S(1)}, bf16[448,768]{1,0:T(8,128)(2,1)S(1)}, u32[]{:S(2)}, u32[]{:S(2)}) %collective-permute-start.16) | collective-permute-done | bytes 688160 | tf_op jit(solution)/shard_map/ppermute | solution.py:70
  54.0 1.5 %shard_map.78 = (bf16[2,416,512]{2,1,0:T(8,128)(2,1)S(1)}, s32[2]{0:T(128)S(1)}) custom-call(s32[2]{0:T(128)S(1)} %copy-done.3, bf16[2,512,128]{2,1,0:T(8,128)(2,1)S(1)} %copy-done.2, bf16[2,512,128]{2,1,0:T(8,128)(2,1)S(1)} %collective-permute-done.8.partner_ref, bf16[2,576,128]{2,1,0:T(8,128)(2,1)S(1)} %collective-permute-done.9.got_ref, ...), custom_call_target="tpu_custom_call" | custom-call | tf_op jit(solution)/shard_map/pallas_call | solution.py:220
  55.5 5.4 %collective-permute-done.12.refs_0_ = bf16[448,768]{1,0:T(8,128)(2,1)S(1)} collective-permute-done((bf16[448,768]{1,0:T(8,128)(2,1)S(1)}, bf16[448,768]{1,0:T(8,128)(2,1)S(1)}, u32[]{:S(2)}, u32[]{:S(2)}) %collective-permute-start.12) | collective-permute-done | bytes 688160 | tf_op jit(solution)/shard_map/ppermute | solution.py:70
  61.6 1.5 %collective-permute-done.14.refs_1_ = bf16[448,768]{1,0:T(8,128)(2,1)S(1)} collective-permute-done((bf16[448,768]{1,0:T(8,128)(2,1)S(1)}, bf16[448,768]{1,0:T(8,128)(2,1)S(1)}, u32[]{:S(2)}, u32[]{:S(2)}) %collective-permute-start.14) | collective-permute-done | bytes 688160 | tf_op jit(solution)/shard_map/ppermute | solution.py:73
  63.3 1.6 %shard_map.81.refs_0_ = bf16[416,1536]{1,0:T(8,128)(2,1)S(1)} custom-call(s32[2]{0:T(128)S(1)} %get-tuple-element.82.lengths_ref, bf16[2,416,512]{2,1,0:T(8,128)(2,1)S(1)} %get-tuple-element.94.grouped_ref, bf16[2,512,768]{2,1,0:T(8,128)(2,1)S(1)} %get-tuple-element.91.weight_ref), custom_call_target="tpu_custom_call" | custom-call | tf_op jit(solution)/shard_map/pallas_call | solution.py:247
  64.8 7.1 %shard_map.82 = bf16[144,1536]{1,0:T(8,128)(2,1)S(1)} custom-call(s32[2]{0:T(128)S(1)} %get-tuple-element.82.lengths_ref, bf16[416,1536]{1,0:T(8,128)(2,1)S(1)} %shard_map.81.refs_0_, f32[2,1536]{1,0:T(2,128)S(1)} %bitcast.10, f32[5,1536]{1,0:T(8,128)S(1)} %bitcast.6, bf16[3,1536,768]{2,1,0:T(8,128)(2,1)S(1)} %get-tuple-element.92.refs_3_.refs_5_, ...), custom_call_target="tpu_custom_call" | custom-call | flops 4130340864 | bytes 9437184 | tf_op jit(solution)/shard_map/pallas_call | solution.py:392
  71.9 1.4 %collective-permute-start.22 = (bf16[144,1536]{1,0:T(8,128)(2,1)S(1)}, bf16[144,1536]{1,0:T(8,128)(2,1)S(1)}, u32[]{:S(2)}, u32[]{:S(2)}) collective-permute-start(bf16[144,1536]{1,0:T(8,128)(2,1)S(1)} %shard_map.82), channel_id=1, source_target_pairs={{0,16},{16,0},{1,17},{17,1},{2,18},{18,2},{3,19},{19,3},{4,20},{20... | collective-permute-start | bytes 1327112 | tf_op jit(solution)/shard_map/ppermute | solution.py:27
  73.3 1.6 %shard_map.83.refs_0_ = bf16[416,1536]{1,0:T(8,128)(2,1)S(1)} custom-call(s32[2]{0:T(128)S(1)} %get-tuple-element.82.lengths_ref, bf16[2,416,512]{2,1,0:T(8,128)(2,1)S(1)} %get-tuple-element.94.grouped_ref, bf16[2,512,768]{2,1,0:T(8,128)(2,1)S(1)} %get-tuple-element.91.weight_ref), custom_call_target="tpu_custom_call" | custom-call | tf_op jit(solution)/shard_map/pallas_call | solution.py:247
  74.8 7.3 %shard_map.84 = bf16[144,1536]{1,0:T(8,128)(2,1)S(1)} custom-call(s32[2]{0:T(128)S(1)} %get-tuple-element.82.lengths_ref, bf16[416,1536]{1,0:T(8,128)(2,1)S(1)} %shard_map.83.refs_0_, f32[2,1536]{1,0:T(2,128)S(1)} %bitcast.11, f32[5,1536]{1,0:T(8,128)S(1)} %bitcast.7, bf16[3,1536,768]{2,1,0:T(8,128)(2,1)S(1)} %get-tuple-element.92.refs_3_.refs_5_, ...), custom_call_target="tpu_custom_call" | custom-call | flops 4130340864 | bytes 9437184 | tf_op jit(solution)/shard_map/pallas_call | solution.py:392
  83.3 5.2 %collective-permute-start.23 = (bf16[144,1536]{1,0:T(8,128)(2,1)S(1)}, bf16[144,1536]{1,0:T(8,128)(2,1)S(1)}, u32[]{:S(2)}, u32[]{:S(2)}) collective-permute-start(bf16[144,1536]{1,0:T(8,128)(2,1)S(1)} %collective-permute-done.22.refs_1_.refs_0_), channel_id=1, source_target_pairs={{0,2},{2,4},{4,6},{6,8},{8,10},{10,12},{12,14},{1,3},{3,5},{5,7},{... | collective-permute-start | bytes 1327112 | tf_op jit(solution)/shard_map/ppermute | solution.py:33
  88.6 1.9 %collective-permute-start.24 = (bf16[144,1536]{1,0:T(8,128)(2,1)S(1)}, bf16[144,1536]{1,0:T(8,128)(2,1)S(1)}, u32[]{:S(2)}, u32[]{:S(2)}) collective-permute-start(bf16[144,1536]{1,0:T(8,128)(2,1)S(1)} %collective-permute-done.22.refs_1_.refs_0_), channel_id=1, source_target_pairs={{2,0},{4,2},{6,4},{8,6},{10,8},{12,10},{14,12},{3,1},{5,3},{7,5},{... | collective-permute-start | bytes 1327112 | tf_op jit(solution)/shard_map/ppermute | solution.py:33
  90.5 2.9 %collective-permute-done.18.refs_1_.refs_0_ = bf16[144,1536]{1,0:T(8,128)(2,1)S(1)} collective-permute-done((bf16[144,1536]{1,0:T(8,128)(2,1)S(1)}, bf16[144,1536]{1,0:T(8,128)(2,1)S(1)}, u32[]{:S(2)}, u32[]{:S(2)}) %collective-permute-start.18) | collective-permute-done | bytes 442400 | tf_op jit(solution)/shard_map/ppermute | solution.py:27
  93.4 5.4 %collective-permute-start.19 = (bf16[144,1536]{1,0:T(8,128)(2,1)S(1)}, bf16[144,1536]{1,0:T(8,128)(2,1)S(1)}, u32[]{:S(2)}, u32[]{:S(2)}) collective-permute-start(bf16[144,1536]{1,0:T(8,128)(2,1)S(1)} %collective-permute-done.18.refs_1_.refs_0_), channel_id=1, source_target_pairs={{0,2},{2,4},{4,6},{6,8},{8,10},{10,12},{12,14},{1,3},{3,5},{5,7},{... | collective-permute-start | bytes 1327112 | tf_op jit(solution)/shard_map/ppermute | solution.py:33
  98.8 1.9 %collective-permute-start.20 = (bf16[144,1536]{1,0:T(8,128)(2,1)S(1)}, bf16[144,1536]{1,0:T(8,128)(2,1)S(1)}, u32[]{:S(2)}, u32[]{:S(2)}) collective-permute-start(bf16[144,1536]{1,0:T(8,128)(2,1)S(1)} %collective-permute-done.18.refs_1_.refs_0_), channel_id=1, source_target_pairs={{2,0},{4,2},{6,4},{8,6},{10,8},{12,10},{14,12},{3,1},{5,3},{7,5},{... | collective-permute-start | bytes 1327112 | tf_op jit(solution)/shard_map/ppermute | solution.py:33
  100.7 6.8 %shard_map.86 = bf16[128,1536]{1,0:T(8,128)(2,1)S(1)} custom-call(s32[2]{0:T(128)S(1)} %get-tuple-element.82.lengths_ref, bf16[144,1536]{1,0:T(8,128)(2,1)S(1)} %collective-permute-done.23.refs_0_, bf16[144,1536]{1,0:T(8,128)(2,1)S(1)} %collective-permute-done.22.refs_1_.refs_0_, bf16[144,1536]{1,0:T(8,128)(2,1)S(1)} %collective-permute-done.24.refs_2_, ...), custom_call_target="tpu_custom_call" | custom-call | flops 4109893632 | bytes 9437184 | tf_op jit(solution)/shard_map/pallas_call | solution.py:392
  108.7 6.8 %shard_map.85 = bf16[128,1536]{1,0:T(8,128)(2,1)S(1)} custom-call(s32[2]{0:T(128)S(1)} %get-tuple-element.82.lengths_ref, bf16[144,1536]{1,0:T(8,128)(2,1)S(1)} %collective-permute-done.19.refs_0_, bf16[144,1536]{1,0:T(8,128)(2,1)S(1)} %collective-permute-done.18.refs_1_.refs_0_, bf16[144,1536]{1,0:T(8,128)(2,1)S(1)} %collective-permute-done.20.refs_2_, ...), custom_call_target="tpu_custom_call" | custom-call | flops 4109893632 | bytes 9437184 | tf_op jit(solution)/shard_map/pallas_call | solution.py:392
  117.4 6.7 %collective-permute-done.21.refs_1_ = bf16[128,1536]{1,0:T(8,128)(2,1)S(1)} collective-permute-done((bf16[128,1536]{1,0:T(8,128)(2,1)S(1)}, bf16[128,1536]{1,0:T(8,128)(2,1)S(1)}, u32[]{:S(2)}, u32[]{:S(2)}) %collective-permute-start.21) | collective-permute-done | bytes 393248 | tf_op jit(solution)/shard_map/ppermute | solution.py:27
  (49 shorter events, 13.5 us)
Async XLA Ops:
  2.1 2.8 %collective-permute-start.2 = (bf16[448,768]{1,0:T(8,128)(2,1)}, bf16[448,768]{1,0:T(8,128)(2,1)S(1)}, u32[]{:S(2)}, u32[]{:S(2)}) collective-permute-start(bf16[448,768]{1,0:T(8,128)(2,1)} %shard_map.73.refs_0_), channel_id=1, source_target_pairs={{0,2},{2,0},{4,6},{6,4},{8,10},{10,8},{12,14},{14,12},{1,3},{3,1},... | collective-permute-start | bytes 2064392 | tf_op jit(solution)/shard_map/ppermute | solution.py:49
  2.2 11.6 %collective-permute-start = (bf16[448,768]{1,0:T(8,128)(2,1)}, bf16[448,768]{1,0:T(8,128)(2,1)S(1)}, u32[]{:S(2)}, u32[]{:S(2)}) collective-permute-start(bf16[448,768]{1,0:T(8,128)(2,1)} %shard_map.73.refs_0_), channel_id=1, source_target_pairs={{0,4},{4,8},{8,12},{12,13},{13,9},{9,5},{5,1},{1,0},{2,3},{6,2},{1... | collective-permute-start | bytes 2064392 | tf_op jit(solution)/shard_map/ppermute | solution.py:70
  4.8 16.3 %collective-permute-start.4 = (bf16[448,768]{1,0:T(8,128)(2,1)S(1)}, bf16[448,768]{1,0:T(8,128)(2,1)S(1)}, u32[]{:S(2)}, u32[]{:S(2)}) collective-permute-start(bf16[448,768]{1,0:T(8,128)(2,1)S(1)} %collective-permute-done.2.refs_1_), channel_id=1, source_target_pairs={{0,4},{4,8},{8,12},{12,13},{13,9},{9,5},{5,1},{1,0},{2,3},{6,2},{1... | collective-permute-start | bytes 2064392 | tf_op jit(solution)/shard_map/ppermute | solution.py:70
  6.8 2.1 %collective-permute-start.8 = (bf16[2,512,128]{2,1,0:T(8,128)(2,1)}, bf16[2,512,128]{2,1,0:T(8,128)(2,1)S(1)}, u32[]{:S(2)}, u32[]{:S(2)}) collective-permute-start(bf16[2,512,128]{2,1,0:T(8,128)(2,1)} %own_ref.1), channel_id=1, source_target_pairs={{0,2},{2,0},{4,6},{6,4},{8,10},{10,8},{12,14},{14,12},{1,3},{3,1},... | collective-permute-start | bytes 786440 | tf_op jit(solution)/shard_map/ppermute | solution.py:476
  8.9 0.9 copy-start.1
  9.9 14.4 %collective-permute-start.9 = (bf16[2,576,128]{2,1,0:T(8,128)(2,1)S(1)}, bf16[2,576,128]{2,1,0:T(8,128)(2,1)S(1)}, u32[]{:S(2)}, u32[]{:S(2)}) collective-permute-start(bf16[2,576,128]{2,1,0:T(8,128)(2,1)S(1)} %shard_map.74), channel_id=1, source_target_pairs={{0,4},{4,8},{8,12},{6,2},{10,6},{14,10},{1,5},{5,9},{9,13},{7,3},{... | collective-permute-start | bytes 884744 | tf_op jit(solution)/shard_map/ppermute | solution.py:478
  13.8 17.9 %collective-permute-start.1 = (bf16[448,768]{1,0:T(8,128)(2,1)S(1)}, bf16[448,768]{1,0:T(8,128)(2,1)S(1)}, u32[]{:S(2)}, u32[]{:S(2)}) collective-permute-start(bf16[448,768]{1,0:T(8,128)(2,1)S(1)} %collective-permute-done.refs_2_), channel_id=1, source_target_pairs={{0,4},{4,8},{8,12},{12,13},{13,9},{9,5},{5,1},{1,0},{2,3},{6,2},{1... | collective-permute-start | bytes 2064392 | tf_op jit(solution)/shard_map/ppermute | solution.py:70
  15.1 16.7 %collective-permute-start.3 = (bf16[448,768]{1,0:T(8,128)(2,1)S(1)}, bf16[448,768]{1,0:T(8,128)(2,1)S(1)}, u32[]{:S(2)}, u32[]{:S(2)}) collective-permute-start(bf16[448,768]{1,0:T(8,128)(2,1)S(1)} %collective-permute-done.refs_2_), channel_id=1, source_target_pairs={{0,2},{2,0},{4,6},{6,4},{8,10},{10,8},{12,14},{14,12},{1,3},{3,1},... | collective-permute-start | bytes 2064392 | tf_op jit(solution)/shard_map/ppermute | solution.py:73
  21.1 10.7 %collective-permute-start.5 = (bf16[448,768]{1,0:T(8,128)(2,1)S(1)}, bf16[448,768]{1,0:T(8,128)(2,1)S(1)}, u32[]{:S(2)}, u32[]{:S(2)}) collective-permute-start(bf16[448,768]{1,0:T(8,128)(2,1)S(1)} %collective-permute-done.4.refs_4_), channel_id=1, source_target_pairs={{0,2},{2,0},{4,6},{6,4},{8,10},{10,8},{12,14},{14,12},{1,3},{3,1},... | collective-permute-start | bytes 2064392 | tf_op jit(solution)/shard_map/ppermute | solution.py:73
  24.3 14.7 %collective-permute-start.10 = (bf16[448,768]{1,0:T(8,128)(2,1)S(1)}, bf16[448,768]{1,0:T(8,128)(2,1)S(1)}, u32[]{:S(2)}, u32[]{:S(2)}) collective-permute-start(bf16[448,768]{1,0:T(8,128)(2,1)S(1)} %collective-permute-done.4.refs_4_), channel_id=1, source_target_pairs={{0,4},{4,8},{8,12},{12,13},{13,9},{9,5},{5,1},{1,0},{2,3},{6,2},{1... | collective-permute-start | bytes 2064392 | tf_op jit(solution)/shard_map/ppermute | solution.py:70
  31.7 11.1 %collective-permute-start.7 = (bf16[448,768]{1,0:T(8,128)(2,1)S(1)}, bf16[448,768]{1,0:T(8,128)(2,1)S(1)}, u32[]{:S(2)}, u32[]{:S(2)}) collective-permute-start(bf16[448,768]{1,0:T(8,128)(2,1)S(1)} %collective-permute-done.1.refs_0_), channel_id=1, source_target_pairs={{0,2},{2,0},{4,6},{6,4},{8,10},{10,8},{12,14},{14,12},{1,3},{3,1},... | collective-permute-start | bytes 2064392 | tf_op jit(solution)/shard_map/ppermute | solution.py:73
  31.8 14.6 %collective-permute-start.6 = (bf16[448,768]{1,0:T(8,128)(2,1)S(1)}, bf16[448,768]{1,0:T(8,128)(2,1)S(1)}, u32[]{:S(2)}, u32[]{:S(2)}) collective-permute-start(bf16[448,768]{1,0:T(8,128)(2,1)S(1)} %collective-permute-done.1.refs_0_), channel_id=1, source_target_pairs={{0,4},{4,8},{8,12},{12,13},{13,9},{9,5},{5,1},{1,0},{2,3},{6,2},{1... | collective-permute-start | bytes 2064392 | tf_op jit(solution)/shard_map/ppermute | solution.py:70
  39.0 7.4 %collective-permute-start.11 = (bf16[448,768]{1,0:T(8,128)(2,1)S(1)}, bf16[448,768]{1,0:T(8,128)(2,1)S(1)}, u32[]{:S(2)}, u32[]{:S(2)}) collective-permute-start(bf16[448,768]{1,0:T(8,128)(2,1)S(1)} %collective-permute-done.10.refs_2_), channel_id=1, source_target_pairs={{0,2},{2,0},{4,6},{6,4},{8,10},{10,8},{12,14},{14,12},{1,3},{3,1},... | collective-permute-start | bytes 2064392 | tf_op jit(solution)/shard_map/ppermute | solution.py:73
  39.2 1.1 copy-start
  40.6 13.1 %collective-permute-start.16 = (bf16[448,768]{1,0:T(8,128)(2,1)S(1)}, bf16[448,768]{1,0:T(8,128)(2,1)S(1)}, u32[]{:S(2)}, u32[]{:S(2)}) collective-permute-start(bf16[448,768]{1,0:T(8,128)(2,1)S(1)} %collective-permute-done.10.refs_2_), channel_id=1, source_target_pairs={{0,4},{4,8},{8,12},{12,13},{13,9},{9,5},{5,1},{1,0},{2,3},{6,2},{1... | collective-permute-start | bytes 2064392 | tf_op jit(solution)/shard_map/ppermute | solution.py:70
  46.4 7.6 %copy-start.2 = (bf16[2,512,128]{2,1,0:T(8,128)(2,1)S(1)}, bf16[2,512,128]{2,1,0:T(8,128)(2,1)}, u32[]{:S(2)}) copy-start(bf16[2,512,128]{2,1,0:T(8,128)(2,1)} %own_ref.1) | copy-start | bytes 786436
  46.4 7.6 %copy-start.3 = (s32[2]{0:T(128)S(1)}, s32[2]{0:T(128)}, u32[]{:S(2)}) copy-start(s32[2]{0:T(128)} %lengths_ref.1) | copy-start | bytes 28
  46.4 14.9 %copy-start.5 = (f32[1,5,1536]{2,0,1:T(1,128)S(1)}, f32[1,5,1536]{2,0,1:T(1,128)}, u32[]{:S(2)}) copy-start(f32[1,5,1536]{2,0,1:T(1,128)} %param.13) | copy-start | bytes 92164
  46.6 14.2 %collective-permute-start.12 = (bf16[448,768]{1,0:T(8,128)(2,1)S(1)}, bf16[448,768]{1,0:T(8,128)(2,1)S(1)}, u32[]{:S(2)}, u32[]{:S(2)}) collective-permute-start(bf16[448,768]{1,0:T(8,128)(2,1)S(1)} %collective-permute-done.6.refs_0_), channel_id=1, source_target_pairs={{0,4},{4,8},{8,12},{12,13},{13,9},{9,5},{5,1},{1,0},{2,3},{6,2},{1... | collective-permute-start | bytes 2064392 | tf_op jit(solution)/shard_map/ppermute | solution.py:70
  47.2 6.8 %collective-permute-start.13 = (bf16[2,64,128]{2,1,0:T(8,128)(2,1)S(1)}, bf16[2,64,128]{2,1,0:T(8,128)(2,1)S(1)}, u32[]{:S(2)}, u32[]{:S(2)}) collective-permute-start(bf16[2,64,128]{2,1,0:T(8,128)(2,1)S(1)} %shard_map.77), channel_id=1, source_target_pairs={{0,2},{2,0},{4,6},{6,4},{8,10},{10,8},{12,14},{14,12},{1,3},{3,1},... | collective-permute-start | bytes 98312 | tf_op jit(solution)/shard_map/ppermute | solution.py:483
  49.4 12.0 %collective-permute-start.15 = (bf16[448,768]{1,0:T(8,128)(2,1)S(1)}, bf16[448,768]{1,0:T(8,128)(2,1)S(1)}, u32[]{:S(2)}, u32[]{:S(2)}) collective-permute-start(bf16[448,768]{1,0:T(8,128)(2,1)S(1)} %collective-permute-done.6.refs_0_), channel_id=1, source_target_pairs={{0,2},{2,0},{4,6},{6,4},{8,10},{10,8},{12,14},{14,12},{1,3},{3,1},... | collective-permute-start | bytes 2064392 | tf_op jit(solution)/shard_map/ppermute | solution.py:73
  53.8 7.6 %collective-permute-start.17 = (bf16[448,768]{1,0:T(8,128)(2,1)S(1)}, bf16[448,768]{1,0:T(8,128)(2,1)S(1)}, u32[]{:S(2)}, u32[]{:S(2)}) collective-permute-start(bf16[448,768]{1,0:T(8,128)(2,1)S(1)} %collective-permute-done.16.refs_2_), channel_id=1, source_target_pairs={{0,2},{2,0},{4,6},{6,4},{8,10},{10,8},{12,14},{14,12},{1,3},{3,1},... | collective-permute-start | bytes 2064392 | tf_op jit(solution)/shard_map/ppermute | solution.py:73
  60.9 2.2 %collective-permute-start.14 = (bf16[448,768]{1,0:T(8,128)(2,1)S(1)}, bf16[448,768]{1,0:T(8,128)(2,1)S(1)}, u32[]{:S(2)}, u32[]{:S(2)}) collective-permute-start(bf16[448,768]{1,0:T(8,128)(2,1)S(1)} %collective-permute-done.12.refs_0_), channel_id=1, source_target_pairs={{0,2},{2,0},{4,6},{6,4},{8,10},{10,8},{12,14},{14,12},{1,3},{3,1},... | collective-permute-start | bytes 2064392 | tf_op jit(solution)/shard_map/ppermute | solution.py:73
  63.2 1.6 %copy-start.4 = (f32[1,2,1536]{2,1,0:T(2,128)S(1)}, f32[1,2,1536]{2,1,0:T(2,128)}, u32[]{:S(2)}) copy-start(f32[1,2,1536]{2,1,0:T(2,128)} %param.12) | copy-start | bytes 36868
  71.9 11.4 %collective-permute-start.22 = (bf16[144,1536]{1,0:T(8,128)(2,1)S(1)}, bf16[144,1536]{1,0:T(8,128)(2,1)S(1)}, u32[]{:S(2)}, u32[]{:S(2)}) collective-permute-start(bf16[144,1536]{1,0:T(8,128)(2,1)S(1)} %shard_map.82), channel_id=1, source_target_pairs={{0,16},{16,0},{1,17},{17,1},{2,18},{18,2},{3,19},{19,3},{4,20},{20... | collective-permute-start | bytes 1327112 | tf_op jit(solution)/shard_map/ppermute | solution.py:27
  82.2 11.2 %collective-permute-start.18 = (bf16[144,1536]{1,0:T(8,128)(2,1)S(1)}, bf16[144,1536]{1,0:T(8,128)(2,1)S(1)}, u32[]{:S(2)}, u32[]{:S(2)}) collective-permute-start(bf16[144,1536]{1,0:T(8,128)(2,1)S(1)} %shard_map.84), channel_id=1, source_target_pairs={{0,16},{16,0},{1,17},{17,1},{2,18},{18,2},{3,19},{19,3},{4,20},{20... | collective-permute-start | bytes 1327112 | tf_op jit(solution)/shard_map/ppermute | solution.py:27
  83.3 17.4 %collective-permute-start.23 = (bf16[144,1536]{1,0:T(8,128)(2,1)S(1)}, bf16[144,1536]{1,0:T(8,128)(2,1)S(1)}, u32[]{:S(2)}, u32[]{:S(2)}) collective-permute-start(bf16[144,1536]{1,0:T(8,128)(2,1)S(1)} %collective-permute-done.22.refs_1_.refs_0_), channel_id=1, source_target_pairs={{0,2},{2,4},{4,6},{6,8},{8,10},{10,12},{12,14},{1,3},{3,5},{5,7},{... | collective-permute-start | bytes 1327112 | tf_op jit(solution)/shard_map/ppermute | solution.py:33
  88.6 12.2 %collective-permute-start.24 = (bf16[144,1536]{1,0:T(8,128)(2,1)S(1)}, bf16[144,1536]{1,0:T(8,128)(2,1)S(1)}, u32[]{:S(2)}, u32[]{:S(2)}) collective-permute-start(bf16[144,1536]{1,0:T(8,128)(2,1)S(1)} %collective-permute-done.22.refs_1_.refs_0_), channel_id=1, source_target_pairs={{2,0},{4,2},{6,4},{8,6},{10,8},{12,10},{14,12},{3,1},{5,3},{7,5},{... | collective-permute-start | bytes 1327112 | tf_op jit(solution)/shard_map/ppermute | solution.py:33
  93.4 14.8 %collective-permute-start.19 = (bf16[144,1536]{1,0:T(8,128)(2,1)S(1)}, bf16[144,1536]{1,0:T(8,128)(2,1)S(1)}, u32[]{:S(2)}, u32[]{:S(2)}) collective-permute-start(bf16[144,1536]{1,0:T(8,128)(2,1)S(1)} %collective-permute-done.18.refs_1_.refs_0_), channel_id=1, source_target_pairs={{0,2},{2,4},{4,6},{6,8},{8,10},{10,12},{12,14},{1,3},{3,5},{5,7},{... | collective-permute-start | bytes 1327112 | tf_op jit(solution)/shard_map/ppermute | solution.py:33
  98.8 9.9 %collective-permute-start.20 = (bf16[144,1536]{1,0:T(8,128)(2,1)S(1)}, bf16[144,1536]{1,0:T(8,128)(2,1)S(1)}, u32[]{:S(2)}, u32[]{:S(2)}) collective-permute-start(bf16[144,1536]{1,0:T(8,128)(2,1)S(1)} %collective-permute-done.18.refs_1_.refs_0_), channel_id=1, source_target_pairs={{2,0},{4,2},{6,4},{8,6},{10,8},{12,10},{14,12},{3,1},{5,3},{7,5},{... | collective-permute-start | bytes 1327112 | tf_op jit(solution)/shard_map/ppermute | solution.py:33
  107.5 9.1 %collective-permute-start.25 = (bf16[128,1536]{1,0:T(8,128)(2,1)S(1)}, bf16[128,1536]{1,0:T(8,128)(2,1)S(1)}, u32[]{:S(2)}, u32[]{:S(2)}) collective-permute-start(bf16[128,1536]{1,0:T(8,128)(2,1)S(1)} %shard_map.86), channel_id=1, source_target_pairs={{0,16},{16,0},{1,17},{17,1},{2,18},{18,2},{3,19},{19,3},{4,20},{20... | collective-permute-start | bytes 1179656 | tf_op jit(solution)/shard_map/ppermute | solution.py:27
  115.5 8.6 %collective-permute-start.21 = (bf16[128,1536]{1,0:T(8,128)(2,1)S(1)}, bf16[128,1536]{1,0:T(8,128)(2,1)S(1)}, u32[]{:S(2)}, u32[]{:S(2)}) collective-permute-start(bf16[128,1536]{1,0:T(8,128)(2,1)S(1)} %shard_map.85), channel_id=1, source_target_pairs={{0,16},{16,0},{1,17},{17,1},{2,18},{18,2},{3,19},{19,3},{4,20},{20... | collective-permute-start | bytes 1179656 | tf_op jit(solution)/shard_map/ppermute | solution.py:27
